TPU v7x, 256 devices: a whole 4x4x8 slice. The times are simulated.
256 devices in a mesh: az: 32 (over z_hi, y, x), rad: 8 (over z_lo, core).
Axes of the slice: x: 4, y: 4, z: 8 (z_hi: 2, z_lo: 4; z = z_hi * 4 + z_lo), core: 2. Of those that a mesh axis runs over, the one named last changes fastest.
Arguments:
- density: float32 [2, 2048, 16384], P(None, 'rad', 'az'), may hold values from 0.5 to 2
- mom_r: float32 [2, 2048, 16384], P(None, 'rad', 'az'), may hold values from -1 to 1
- mom_phi: float32 [2, 2048, 16384], P(None, 'rad', 'az'), may hold values from 0.5 to 1.5
- potential_kernel: bfloat16 [64, 2048, 2048], P('az', 'rad'), may hold values from -2 to 2
- force_kernel: bfloat16 [64, 2048, 2048], P('az', 'rad'), may hold values from -2 to 2
Outputs:
- new_density: float32 [2, 2048, 16384], P(None, 'rad', 'az')
- new_mom_r: float32 [2, 2048, 16384], P(None, 'rad', 'az')
- new_mom_phi: float32 [2, 2048, 16384], P(None, 'rad', 'az')
- potential: float32 [2048, 16384], P('rad', 'az')
All inputs are finite; a program needn't handle non-finite values.
Results may differ from a plain program's by a relative error of at most 0.0015.
The roundings to bfloat16 on the way count: a program that leaves them out, or rounds other values in their place, can miss the bound.
Values may be sent and summed in bfloat16 or wider, within the bound.
A program may use at most 128 MiB of HBM per device.

v0:
```python
import math
import jax
import jax.numpy as jnp
from jax import lax
from jax.sharding import PartitionSpec as P

NAZ = 16384
MODES = 64
aspect_sq = 0.0025


def in_blocks(shard, dim, size):
    before, after = (shard.shape[:dim], shard.shape[dim + 1 :])
    return jnp.moveaxis(shard.reshape(*before, size, -1, *after), dim, 0)


def sum_at_owner(shard, axis, dim):
    blocks = in_blocks(shard, dim, lax.axis_size(axis))
    arrived = lax.all_to_all(blocks, axis, split_axis=0, concat_axis=0, tiled=True)
    return arrived.sum(axis=0)


def laid_out(blocks, dim):
    lengths = list(blocks.shape[1:])
    lengths[dim] *= blocks.shape[0]
    return jnp.moveaxis(blocks, 0, dim).reshape(lengths)


def copy_for_each(shard, axis):
    size = lax.axis_size(axis)
    return lax.all_to_all(
        jnp.broadcast_to(shard[None], (size, *shard.shape)), axis, 0, 0, tiled=True
    )


def gathered_copies(shard, axis, dim):
    return laid_out(copy_for_each(shard, axis), dim)


def rows_first(arrays, axis, dims):
    turned = [jnp.moveaxis(a, dim, 0) for a, dim in zip(arrays, dims)]
    both = jnp.concatenate([t.reshape(len(t), -1) for t in turned], axis=1)
    result, at, gathered = (lax.all_gather(both, axis, axis=0, tiled=True), 0, [])
    for t, dim in zip(turned, dims):
        slab = result[:, at : at + t[0].size].reshape(-1, *t.shape[1:])
        gathered.append(jnp.moveaxis(slab, 0, dim))
        at += t[0].size
    return tuple(gathered)


def extended(block, sides, width, periodic):
    for axis, dim in sides:
        count = lax.axis_size(axis)
        forward = [(i, i + 1) for i in range(count - 1)]
        if periodic:
            forward.append((count - 1, 0))
        backward = [(target, source) for source, target in forward]
        low = lax.ppermute(
            lax.slice_in_dim(block, block.shape[dim] - width, None, axis=dim), axis, forward
        )
        high = lax.ppermute(lax.slice_in_dim(block, 0, width, axis=dim), axis, backward)
        block = jnp.concatenate([low, block, high], axis=dim)
    return block


def mode_table(azimuth):
    mode_index = jnp.arange(MODES).astype(jnp.float32)
    angles = azimuth[:, None] * mode_index[None, :]
    basis = jnp.stack([jnp.cos(angles), jnp.sin(angles)], axis=-1).reshape(
        azimuth.shape[0], 2 * MODES
    )
    slope = jnp.stack(
        [-mode_index * jnp.sin(angles), mode_index * jnp.cos(angles)], axis=-1
    ).reshape(azimuth.shape[0], 2 * MODES)
    return (basis, slope)


def radial_flux(lower_side, upper_side, sound):

    def physical(fields):
        velocity = fields[1] / fields[0]
        flux = jnp.stack(
            [fields[1], fields[1] * velocity + sound * fields[0], fields[2] * velocity]
        )
        return (flux, velocity)

    flux_lower, vel_lower = physical(lower_side)
    flux_upper, vel_upper = physical(upper_side)
    wave_speed = jnp.maximum(jnp.abs(vel_lower), jnp.abs(vel_upper)) + jnp.sqrt(sound)
    return 0.5 * (flux_lower + flux_upper) - 0.5 * wave_speed * (upper_side - lower_side)


def azimuth_flux(lower_side, upper_side, sound):

    def physical(fields):
        velocity = fields[2] / fields[0]
        flux = jnp.stack(
            [fields[2], fields[1] * velocity, fields[2] * velocity + sound * fields[0]]
        )
        return (flux, velocity)

    flux_lower, vel_lower = physical(lower_side)
    flux_upper, vel_upper = physical(upper_side)
    wave_speed = jnp.maximum(jnp.abs(vel_lower), jnp.abs(vel_upper)) + jnp.sqrt(sound)
    return 0.5 * (flux_lower + flux_upper) - 0.5 * wave_speed * (upper_side - lower_side)


def tendency(fields, radial_ext, azimuth_ext, face_radius, grav_radial, grav_azimuth, cell_step):
    inner_radius = face_radius[:-1]
    outer_radius = face_radius[1:]
    mid_radius = 0.5 * (inner_radius + outer_radius)
    cell_area = 0.5 * (outer_radius * outer_radius - inner_radius * inner_radius)
    sound_face = (aspect_sq / face_radius)[:, None]
    sound_mid = (aspect_sq / mid_radius)[:, None]
    flux_rad = radial_flux(radial_ext[:, :, :-1], radial_ext[:, :, 1:], sound_face)
    flux_azi = azimuth_flux(azimuth_ext[..., :-1], azimuth_ext[..., 1:], sound_mid)
    weighted = flux_rad * face_radius[:, None]
    divergence = (weighted[:, :, 1:] - weighted[:, :, :-1]) / cell_area[:, None]
    divergence = divergence + (flux_azi[..., 1:] - flux_azi[..., :-1]) / (
        mid_radius[:, None] * cell_step
    )
    surface_now = fields[0]
    radial_mom = fields[1]
    spin_mom = fields[2]
    centre = mid_radius[:, None]
    source_rad = (spin_mom * spin_mom / surface_now + sound_mid * surface_now) / centre
    source_rad = source_rad + surface_now * (grav_radial / cell_step - 1.0 / (centre * centre))
    source_azi = -radial_mom * spin_mom / (surface_now * centre) + surface_now * (
        grav_azimuth / cell_step
    )
    source = jnp.stack([jnp.zeros_like(surface_now), source_rad, source_azi])
    return fields + 0.1 * cell_step * (source - divergence)


def local(density, mom_r, mom_phi, potential_kernel, force_kernel):
    highest = lax.Precision.HIGHEST
    row_count = density.shape[1]
    cell_count = density.shape[2]
    mode_count = potential_kernel.shape[0]
    col_count = 2 * mode_count
    cell_step = 2.0 * math.pi / NAZ
    az_index = lax.axis_index("az")
    rad_index = lax.axis_index("rad")
    azimuth = (
        (az_index * cell_count + jnp.arange(cell_count)).astype(jnp.float32) + 0.5
    ) * cell_step
    basis, slope = mode_table(azimuth)
    surface = jnp.sum(density, axis=0)
    partial_modes = jnp.dot(surface, basis, precision=highest) / NAZ
    own_modes = sum_at_owner(partial_modes, "az", 1)
    own_pairs = own_modes.astype(jnp.bfloat16)
    portion = gathered_copies(own_pairs, "rad", 0)
    count = portion.shape[0]
    pairs = portion.reshape(count, mode_count, 2)
    pot_part = jnp.einsum(
        "krs,skc->rkc", potential_kernel, pairs, preferred_element_type=jnp.float32
    ).reshape(row_count, col_count)
    force_part = jnp.einsum(
        "krs,skc->rkc", force_kernel, pairs, preferred_element_type=jnp.float32
    ).reshape(row_count, col_count)
    basis_rows = basis.T
    slope_rows = slope.T
    portion = rows_first((pot_part, force_part), "az", (1, 1))
    potential = jnp.dot(portion[0], basis_rows, precision=highest)
    grav_radial = jnp.dot(portion[1], basis_rows, precision=highest)
    slope_sum = jnp.dot(portion[0], slope_rows, precision=highest)
    face_radius = jnp.exp(
        (rad_index * row_count + jnp.arange(row_count + 1)).astype(jnp.float32) * cell_step
    )
    mid_radius = 0.5 * (face_radius[:-1] + face_radius[1:])
    grav_azimuth = -slope_sum / mid_radius[:, None]
    fields = jnp.stack([density, mom_r, mom_phi])
    azimuth_ext = extended(fields.astype(jnp.bfloat16), (("az", 3),), 1, True).astype(fields.dtype)
    radial_halo = extended(fields.astype(jnp.bfloat16), (("rad", 2),), 1, False).astype(
        fields.dtype
    )
    inner_rim = jnp.where(rad_index == 0, fields[:, :, :1], radial_halo[:, :, :1])
    outer_rim = jnp.where(
        rad_index == lax.axis_size("rad") - 1, fields[:, :, -1:], radial_halo[:, :, -1:]
    )
    radial_ext = jnp.concatenate([inner_rim, fields, outer_rim], axis=2)
    result = tendency(
        fields, radial_ext, azimuth_ext, face_radius, grav_radial, grav_azimuth, cell_step
    )
    return (result[0], result[1], result[2], potential)


def solution(mesh):
    placed = (
        P(None, "rad", "az"),
        P(None, "rad", "az"),
        P(None, "rad", "az"),
        P("az", "rad", None),
        P("az", "rad", None),
    )
    return jax.shard_map(
        local,
        mesh=mesh,
        in_specs=placed,
        out_specs=(
            P(None, "rad", "az"),
            P(None, "rad", "az"),
            P(None, "rad", "az"),
            P("rad", "az"),
        ),
        check_vma=False,
    )
```

profile of v0, /device:TPU:32, one launch (start us, length us, event | category | flops | bytes accessed | tf_op | source)
XLA Modules:
  0.0 215.3 jit_solution(8879129993631499688)
XLA Ops:
  0.6 2.3 %fusion.22 = bf16[3,2,256,512]{3,2,1,0:T(8,128)(2,1)S(1)} fusion(f32[1,2,256,512]{3,2,1,0:T(8,128)} %bitcast.53, f32[1,2,256,512]{3,2,1,0:T(8,128)} %bitcast.58, f32[1,2,256,512]{3,2,1,0:T(8,128)} %bitcast.48), kind=kLoop, calls=%fused_computation.76 | loop fusion | flops 1572864 | bytes 4718592 | tf_op jit(solution)/shard_map/convert_element_type | solution.py:174
  3.0 1.1 fusion.25
  4.1 10.9 %collective-permute-start.3 = (bf16[3,2,256,1]{3,2,1,0:T(8,128)(2,1)}, bf16[3,2,256,1]{3,2,1,0:T(8,128)(2,1)}, u32[]{:S(2)}, u32[]{:S(2)}) collective-permute-start(bf16[3,2,256,1]{3,2,1,0:T(8,128)(2,1)} %get-tuple-element.34), channel_id=1, source_target_pairs={{8,0},{16,8},{24,16},{32,24},{40,32},{48,40},{56,48},{64,56},{72,6... | collective-permute-start | bytes 9224 | tf_op jit(solution)/shard_map/ppermute | solution.py:61
  15.6 2.1 collective-permute-start.1
  17.7 2.3 %collective-permute-start = (bf16[3,2,1,512]{3,2,1,0:T(2,128)(2,1)}, bf16[3,2,1,512]{3,2,1,0:T(2,128)(2,1)}, u32[]{:S(2)}, u32[]{:S(2)}) collective-permute-start(bf16[3,2,1,512]{3,2,1,0:T(2,128)(2,1)} %get-tuple-element.31), channel_id=1, source_target_pairs={{0,1},{1,2},{2,3},{3,4},{4,5},{5,6},{6,7},{8,9},{9,10},{10,11},{11... | collective-permute-start | bytes 18440 | tf_op jit(solution)/shard_map/ppermute | solution.py:58
  20.6 0.8 pad_maximum_fusion.2
  21.3 0.9 copy.10
  22.2 1.1 reshape.288
  23.4 0.9 reduce_sum.18
  24.3 1.7 convolution_multiply_fusion.1
  26.7 11.8 %all-to-all-start = ((f32[32,256,4]{1,2,0:T(4,128)}), f32[32,256,4]{1,2,0:T(4,128)S(1)}, u32[]{:S(2)}, u32[]{:S(2)}) async-start(f32[32,256,4]{1,2,0:T(4,128)} %bitcast.63), calls=%async_computation | async-start | bytes 262144 | tf_op jit(solution)/shard_map/all_to_all | solution.py:19
  38.5 3.8 %pad_maximum_fusion.1 = f32[3,2,256,512]{3,2,1,0:T(8,128)} fusion(f32[1,2,256,512]{3,2,1,0:T(8,128)} %bitcast.54, f32[1,2,256,512]{3,2,1,0:T(8,128)} %bitcast.59, f32[1,2,256,512]{3,2,1,0:T(8,128)S(1)} %bitcast.49), kind=kLoop, calls=%fused_computation.19 | loop fusion | flops 1572864 | bytes 6291456 | tf_op jit(solution)/shard_map/stack | solution.py:172
  44.7 1.9 copy.12
  46.6 1.8 reshape.292
  49.0 2.5 %maximum_convert_fusion = f32[3,2,256,514]{3,2,1,0:T(8,128)S(1)} fusion(bf16[3,2,256,1]{3,2,1,0:T(8,128)(2,1)} %collective-permute-done.3, bf16[3,2,256,512]{3,2,1,0:T(8,128)(2,1)} %copy-done.8, bf16[3,2,256,1]{3,2,1,0:T(8,128)(2,1)} %collective-permute-done.2), kind=kLoop, calls=%fused_computation.20 | loop fusion | flops 4737024 | bytes 4737024 | tf_op jit(solution)/shard_map/convert_element_type | solution.py:173
  51.4 1.4 multiply_add_fusion
  52.9 2.5 %fusion.1 = f32[3,2,256,513]{3,2,1,0:T(8,128)} fusion(f32[3,2,256,514]{3,2,1,0:T(8,128)S(1)} %maximum_convert_fusion, f32[1,2,256,513]{3,2,1,0:T(8,128)S(1)} %get-tuple-element.11, f32[1,2,256,513]{3,2,1,0:T(8,128)S(1)} %get-tuple-element.15, f32[1,2,256,513]{3,2,1,0:T(8,128)S(1)} %get-tuple-element.16, f32[1,2,256,513]{3,2,1,0:T(8,128)S(1)} %get-tuple-element.10, ...), kind=kLoop, calls=%fused_computation.2 | loop fusion | flops 7091712 | bytes 16809984 | tf_op jit(solution)/shard_map/sub | solution.py:105
  56.0 1.0 broadcast_select_fusion
  57.1 0.8 pad_maximum_fusion
  58.0 4.3 %multiply_bitcast_fusion.1 = (f32[2,257,512]{2,1,0:T(8,128)}, f32[1,2,257,512]{3,2,1,0:T(8,128)}, f32[1,2,257,512]{3,2,1,0:T(8,128)}, f32[1,2,257,512]{3,2,1,0:T...) fusion(f32[257]{0:T(512)S(1)} %copy-done.17, ...), kind=kLoop, calls=%fused_computation.38 | loop fusion | flops 3947520 | bytes 13686792 | tf_op jit(solution)/shard_map/mul | solution.py:90
  62.9 1.3 broadcast_in_dim.2
  64.2 4.8 %all-to-all-start.1 = ((bf16[8,256,4]{1,2,0:T(4,128)(2,1)}), bf16[8,256,4]{1,2,0:T(4,128)(2,1)S(1)}, u32[]{:S(2)}, u32[]{:S(2)}) async-start(bf16[8,256,4]{1,2,0:T(4,128)(2,1)} %broadcast_in_dim.2), calls=%async_computation.1 | async-start | bytes 32768 | tf_op jit(solution)/shard_map/all_to_all | solution.py:31
  69.0 7.4 %fusion.5 = f32[3,2,257,512]{3,2,1,0:T(8,128)} fusion(f32[1,2,257,512]{3,2,1,0:T(8,128)} %get-tuple-element.22, f32[1,2,257,512]{3,2,1,0:T(8,128)} %get-tuple-element.19, f32[1,2,257,512]{3,2,1,0:T(8,128)} %get-tuple-element.23, f32[1,2,257,512]{3,2,1,0:T(8,128)} %get-tuple-element.20, f32[1,2,257,512]{3,2,1,0:T(8,128)} %get-tuple-element.18, ...), kind=kLoop, calls=%fused_computation.9 | loop fusion | flops 12632064 | bytes 13698052 | tf_op jit(solution)/shard_map/mul | solution.py:117
  77.2 2.2 %convolution_bitcast_fusion.1 = f32[256,2,2]{0,2,1:T(2,128)S(1)} fusion(bf16[2048,2,2]{0,2,1:T(2,128)(2,1)S(1)} %reshape_reshape.3, bf16[2,256,2048]{2,1,0:T(8,128)(2,1)} %param.8), kind=kOutput, calls=%fused_computation.35 | convolution fusion | flops 4194304 | bytes 2117632 | tf_op jit(solution)/shard_map/krs,skc->rkc/dot_general | solution.py:155
  79.4 122.8 %all-gather = f32[32,4,512]{2,1,0:T(4,128)} all-gather(f32[1,4,512]{2,1,0:T(4,128)S(1)} %maximum_bitcast_fusion), channel_id=1, replica_groups=mesh['az'=32,'rad'=8] {'az'}, dimensions={0}, use_global_device_ids=true | all-gather | bytes 270336 | tf_op jit(solution)/shard_map/all_gather | solution.py:43
  202.2 1.7 reshape.294
  203.9 2.5 %fusion.16 = f32[256,512]{1,0:T(8,128)} fusion(f32[512,128]{0,1:T(8,128)S(1)} %reshape.288, f32[128,512]{1,0:T(8,128)} %reshape.294), kind=kOutput, calls=%fused_computation.53 | convolution fusion | flops 201326592 | bytes 917504 | tf_op jit(solution)/shard_map/dot_general | solution.py:164
  206.4 1.5 fusion.14
  208.0 1.8 fusion.13
  210.6 1.3 copy-done.6
  211.8 1.7 fusion.10
  213.6 1.7 slice_bitcast_fusion
  (71 shorter events, 7.6 us)
Async XLA Ops:
  0.6 75.8 %copy-start = (bf16[2,256,2048]{2,1,0:T(8,128)(2,1)S(1)}, bf16[2,256,2048]{2,1,0:T(8,128)(2,1)}, u32[]{:S(2)}) copy-start(bf16[2,256,2048]{2,1,0:T(8,128)(2,1)} %param.9) | copy-start | bytes 6291460
  3.0 12.0 %copy-start.8 = (bf16[3,2,256,512]{3,2,1,0:T(8,128)(2,1)}, bf16[3,2,256,512]{3,2,1,0:T(8,128)(2,1)S(1)}, u32[]{:S(2)}) copy-start(bf16[3,2,256,512]{3,2,1,0:T(8,128)(2,1)S(1)} %fusion.22) | copy-start | bytes 4718596
  3.0 20.3 %copy-start.1 = (f32[2,256,512]{2,1,0:T(8,128)S(1)}, f32[2,256,512]{2,1,0:T(8,128)}, u32[]{:S(2)}) copy-start(f32[2,256,512]{2,1,0:T(8,128)} %param.5) | copy-start | bytes 3145732
  4.1 44.9 %collective-permute-start.3 = (bf16[3,2,256,1]{3,2,1,0:T(8,128)(2,1)}, bf16[3,2,256,1]{3,2,1,0:T(8,128)(2,1)}, u32[]{:S(2)}, u32[]{:S(2)}) collective-permute-start(bf16[3,2,256,1]{3,2,1,0:T(8,128)(2,1)} %get-tuple-element.34), channel_id=1, source_target_pairs={{8,0},{16,8},{24,16},{32,24},{40,32},{48,40},{56,48},{64,56},{72,6... | collective-permute-start | bytes 9224 | tf_op jit(solution)/shard_map/ppermute | solution.py:61
  15.0 33.9 %collective-permute-start.2 = (bf16[3,2,256,1]{3,2,1,0:T(8,128)(2,1)}, bf16[3,2,256,1]{3,2,1,0:T(8,128)(2,1)}, u32[]{:S(2)}, u32[]{:S(2)}) collective-permute-start(bf16[3,2,256,1]{3,2,1,0:T(8,128)(2,1)} %get-tuple-element.33), channel_id=1, source_target_pairs={{0,8},{8,16},{16,24},{24,32},{32,40},{40,48},{48,56},{56,64},{64,7... | collective-permute-start | bytes 9224 | tf_op jit(solution)/shard_map/ppermute | solution.py:58
  15.6 39.8 %collective-permute-start.1 = (bf16[3,2,1,512]{3,2,1,0:T(2,128)(2,1)}, bf16[3,2,1,512]{3,2,1,0:T(2,128)(2,1)S(1)}, u32[]{:S(2)}, u32[]{:S(2)}) collective-permute-start(bf16[3,2,1,512]{3,2,1,0:T(2,128)(2,1)} %get-tuple-element.32), channel_id=1, source_target_pairs={{1,0},{2,1},{3,2},{4,3},{5,4},{6,5},{7,6},{9,8},{10,9},{11,10},{12... | collective-permute-start | bytes 18440 | tf_op jit(solution)/shard_map/ppermute | solution.py:61
  17.7 38.3 %collective-permute-start = (bf16[3,2,1,512]{3,2,1,0:T(2,128)(2,1)}, bf16[3,2,1,512]{3,2,1,0:T(2,128)(2,1)}, u32[]{:S(2)}, u32[]{:S(2)}) collective-permute-start(bf16[3,2,1,512]{3,2,1,0:T(2,128)(2,1)} %get-tuple-element.31), channel_id=1, source_target_pairs={{0,1},{1,2},{2,3},{3,4},{4,5},{5,6},{6,7},{8,9},{9,10},{10,11},{11... | collective-permute-start | bytes 18440 | tf_op jit(solution)/shard_map/ppermute | solution.py:58
  26.7 35.6 %all-to-all-start = ((f32[32,256,4]{1,2,0:T(4,128)}), f32[32,256,4]{1,2,0:T(4,128)S(1)}, u32[]{:S(2)}, u32[]{:S(2)}) async-start(f32[32,256,4]{1,2,0:T(4,128)} %bitcast.63), calls=%async_computation | async-start | bytes 262144 | tf_op jit(solution)/shard_map/all_to_all | solution.py:19
  43.0 0.5 copy-start.14
  48.9 2.5 %copy-start.12 = (f32[256]{0:T(256)S(1)}, f32[256]{0:T(256)}, u32[]{:S(2)}) copy-start(f32[256]{0:T(256)} %get-tuple-element.7) | copy-start | bytes 3076
  48.9 2.5 %copy-start.18 = (f32[256]{0:T(256)S(1)}, f32[256]{0:T(256)}, u32[]{:S(2)}) copy-start(f32[256]{0:T(256)} %get-tuple-element.6) | copy-start | bytes 3076
  52.9 3.1 %copy-start.9 = (bf16[3,2,256,512]{3,2,1,0:T(8,128)(2,1)S(1)}, bf16[3,2,256,512]{3,2,1,0:T(8,128)(2,1)}, u32[]{:S(2)}) copy-start(bf16[3,2,256,512]{3,2,1,0:T(8,128)(2,1)} %copy-done.8) | copy-start | bytes 4718596
  52.9 4.2 %copy-start.2 = (f32[2,256,512]{2,1,0:T(8,128)S(1)}, f32[2,256,512]{2,1,0:T(8,128)}, u32[]{:S(2)}) copy-start(f32[2,256,512]{2,1,0:T(8,128)} %param.7) | copy-start | bytes 3145732
  52.9 4.2 %copy-start.4 = (f32[2,256,512]{2,1,0:T(8,128)S(1)}, f32[2,256,512]{2,1,0:T(8,128)}, u32[]{:S(2)}) copy-start(f32[2,256,512]{2,1,0:T(8,128)} %param.6) | copy-start | bytes 3145732
  55.4 0.6 copy-start.11
  57.0 0.9 copy-start.10
  57.1 0.9 copy-start.16
  57.1 0.9 copy-start.17
  64.2 12.2 %all-to-all-start.1 = ((bf16[8,256,4]{1,2,0:T(4,128)(2,1)}), bf16[8,256,4]{1,2,0:T(4,128)(2,1)S(1)}, u32[]{:S(2)}, u32[]{:S(2)}) async-start(bf16[8,256,4]{1,2,0:T(4,128)(2,1)} %broadcast_in_dim.2), calls=%async_computation.1 | async-start | bytes 32768 | tf_op jit(solution)/shard_map/all_to_all | solution.py:31
  76.4 130.0 %copy-start.21 = (f32[256]{0:T(256)S(1)}, f32[256]{0:T(256)}, u32[]{:S(2)}) copy-start(f32[256]{0:T(256)} %get-tuple-element.41) | copy-start | bytes 3076
  76.5 131.5 %copy-start.15 = (f32[256]{0:T(256)S(1)}, f32[256]{0:T(256)}, u32[]{:S(2)}) copy-start(f32[256]{0:T(256)} %copy-done.14) | copy-start | bytes 3076
  77.1 132.6 %copy-start.13 = (f32[256]{0:T(256)S(1)}, f32[256]{0:T(256)}, u32[]{:S(2)}) copy-start(f32[256]{0:T(256)} %get-tuple-element.7) | copy-start | bytes 3076
  203.9 5.9 %copy-start.3 = (f32[2,256,512]{2,1,0:T(8,128)S(1)}, f32[2,256,512]{2,1,0:T(8,128)}, u32[]{:S(2)}) copy-start(f32[2,256,512]{2,1,0:T(8,128)} %param.7) | copy-start | bytes 3145732
  203.9 5.9 %copy-start.5 = (f32[2,256,512]{2,1,0:T(8,128)S(1)}, f32[2,256,512]{2,1,0:T(8,128)}, u32[]{:S(2)}) copy-start(f32[2,256,512]{2,1,0:T(8,128)} %param.6) | copy-start | bytes 3145732
  207.9 2.6 %copy-start.7 = (f32[3,2,256,513]{3,2,1,0:T(8,128)S(1)}, f32[3,2,256,513]{3,2,1,0:T(8,128)}, u32[]{:S(2)}) copy-start(f32[3,2,256,513]{3,2,1,0:T(8,128)} %fusion.1) | copy-start | bytes 9455620
  209.8 2.0 copy-start.6
  209.8 2.0 copy-start.19
  209.8 2.0 copy-start.20
  209.8 2.0 copy-start.22
where the time goes:
time: 216 us; the launch traced here: 215 us
  blocking collectives  123 us (57%)
  other arithmetic  33.3 us (15%)
  starting transfers between devices  31.9 us (15%)
  local copies, waits for them, and re-layouts  15.9 us (7%)
  matrix products  10.4 us (5%)
    all_gather x1, blocking collectives, rows_first(): lax.all_gather(both, axis, axis=0, tiled=True)  123 us
    ppermute x2, starting transfers between devices, extended(): lax.ppermute(lax.slice_in_dim(block, 0, width, axis=dim), axis, backward)  13 us
    all_to_all x1, starting transfers between devices, sum_at_owner(): lax.all_to_all(blocks, axis, split_axis=0, concat_axis=0, tiled=True)  11.8 us
    mul x1, other arithmetic, tendency(): weighted = flux_rad * face_radius[:, None]  7.43 us
    all_to_all x1, starting transfers between devices, copy_for_each(): lax.all_to_all(jnp.broadcast_to(shard[None], (size, *shard.shape)), axis,...  4.81 us
  transfers between devices with their start and end apart: 6, of which 0 were waited for; matrix products, arithmetic and copies ran while one was open for 17% of the time, Pallas kernels for 0%

commit v1 on v0

--- a/solution.py
+++ b/solution.py
@@ -40,7 +40,13 @@
 def rows_first(arrays, axis, dims):
     turned = [jnp.moveaxis(a, dim, 0) for a, dim in zip(arrays, dims)]
     both = jnp.concatenate([t.reshape(len(t), -1) for t in turned], axis=1)
-    result, at, gathered = (lax.all_gather(both, axis, axis=0, tiled=True), 0, [])
+    result, at, gathered = (
+        jnp.concatenate(
+            lax.all_to_all(jnp.stack([both] * lax.axis_size(axis), axis=0), axis, 0, 0), axis=0
+        ),
+        0,
+        [],
+    )
     for t, dim in zip(turned, dims):
         slab = result[:, at : at + t[0].size].reshape(-1, *t.shape[1:])
         gathered.append(jnp.moveaxis(slab, 0, dim))

time: 216 us -> 121 us (0.56)
  blocking collectives: 123 us -> 0 us
  starting transfers between devices: 31.9 us -> 44.4 us
  waiting for transfers between devices: 0.02 us -> 8.46 us
  other arithmetic: 33.3 us -> 38.5 us
    all_gather x1 -> x0, blocking collectives: 123 us -> none  [rows_first(): lax.all_gather(both, axis, axis=0, tiled=True)]
    all_to_all x0 -> x1, starting transfers between devices: none -> 12.5 us  [rows_first(): lax.all_to_all(jnp.stack([both] * lax.axis_size(axis), axis=0), axis, 0, 0)]
    all_to_all x0 -> x1, waiting for transfers between devices: none -> 8.44 us  [rows_first(): lax.all_to_all(jnp.stack([both] * lax.axis_size(axis), axis=0), axis, 0, 0)]
    mul x1, other arithmetic: 4.3 us -> 7.27 us  [radial_flux(): 0.5 * wave_speed * (upper_side - lower_side)]
    concatenate x1, other arithmetic: 0.84 us -> 3.14 us  [local(): radial_ext = jnp.concatenate([inner_rim, fields, outer_rim], axis=2)]
  transfers between devices with their start and end apart: 6 -> 7, of which waited for: 0 -> 1; matrix products, arithmetic and copies ran while one was open for 17% -> 35% of each run, Pallas kernels for 0% -> 0%
where the time goes in v1:
time: 121 us; the launch traced here: 120 us
  starting transfers between devices  44.4 us (37%)
  other arithmetic  38.5 us (32%)
  local copies, waits for them, and re-layouts  17.3 us (14%)
  matrix products  10.4 us (9%)
  waiting for transfers between devices  8.46 us (7%)
    ppermute x2, starting transfers between devices, extended(): lax.ppermute(lax.slice_in_dim(block, 0, width, axis=dim), axis, backward)  13 us
    all_to_all x1, starting transfers between devices, rows_first(): lax.all_to_all(jnp.stack([both] * lax.axis_size(axis), axis=0), axis, 0, 0)  12.5 us
    all_to_all x1, starting transfers between devices, sum_at_owner(): lax.all_to_all(blocks, axis, split_axis=0, concat_axis=0, tiled=True)  11.8 us
    all_to_all x1, waiting for transfers between devices, rows_first(): lax.all_to_all(jnp.stack([both] * lax.axis_size(axis), axis=0), axis, 0, 0)  8.44 us
    mul x1, other arithmetic, tendency(): weighted = flux_rad * face_radius[:, None]  7.39 us
    mul x1, other arithmetic, radial_flux(): 0.5 * wave_speed * (upper_side - lower_side)  7.27 us
    all_to_all x1, starting transfers between devices, copy_for_each(): lax.all_to_all(jnp.broadcast_to(shard[None], (size, *shard.shape)), axis,...  4.8 us
    another operation x1, other arithmetic, local(): fields = jnp.stack([density, mom_r, mom_phi])  3.81 us
  transfers between devices with their start and end apart: 7, of which 1 were waited for; matrix products, arithmetic and copies ran while one was open for 35% of the time, Pallas kernels for 0%

profile of v1, /device:TPU:32, one launch (start us, length us, event | category | flops | bytes accessed | tf_op | source)
XLA Modules:
  0.0 120.1 jit_solution(7119657811053148488)
XLA Ops:
  0.6 2.3 %fusion.22 = bf16[3,2,256,512]{3,2,1,0:T(8,128)(2,1)S(1)} fusion(f32[1,2,256,512]{3,2,1,0:T(8,128)} %bitcast.51, f32[1,2,256,512]{3,2,1,0:T(8,128)} %bitcast.56, f32[1,2,256,512]{3,2,1,0:T(8,128)} %bitcast.46), kind=kLoop, calls=%fused_computation.76 | loop fusion | flops 1572864 | bytes 4718592 | tf_op jit(solution)/shard_map/convert_element_type | solution.py:180
  3.0 1.1 fusion.25
  4.1 10.9 %collective-permute-start.3 = (bf16[3,2,256,1]{3,2,1,0:T(8,128)(2,1)}, bf16[3,2,256,1]{3,2,1,0:T(8,128)(2,1)}, u32[]{:S(2)}, u32[]{:S(2)}) collective-permute-start(bf16[3,2,256,1]{3,2,1,0:T(8,128)(2,1)} %get-tuple-element.34), channel_id=1, source_target_pairs={{8,0},{16,8},{24,16},{32,24},{40,32},{48,40},{56,48},{64,56},{72,6... | collective-permute-start | bytes 9224 | tf_op jit(solution)/shard_map/ppermute | solution.py:67
  15.6 2.1 %collective-permute-start.1 = (bf16[3,2,1,512]{3,2,1,0:T(2,128)(2,1)}, bf16[3,2,1,512]{3,2,1,0:T(2,128)(2,1)S(1)}, u32[]{:S(2)}, u32[]{:S(2)}) collective-permute-start(bf16[3,2,1,512]{3,2,1,0:T(2,128)(2,1)} %get-tuple-element.32), channel_id=1, source_target_pairs={{1,0},{2,1},{3,2},{4,3},{5,4},{6,5},{7,6},{9,8},{10,9},{11,10},{12... | collective-permute-start | bytes 18440 | tf_op jit(solution)/shard_map/ppermute | solution.py:67
  17.7 2.3 %collective-permute-start = (bf16[3,2,1,512]{3,2,1,0:T(2,128)(2,1)}, bf16[3,2,1,512]{3,2,1,0:T(2,128)(2,1)}, u32[]{:S(2)}, u32[]{:S(2)}) collective-permute-start(bf16[3,2,1,512]{3,2,1,0:T(2,128)(2,1)} %get-tuple-element.31), channel_id=1, source_target_pairs={{0,1},{1,2},{2,3},{3,4},{4,5},{5,6},{6,7},{8,9},{9,10},{10,11},{11... | collective-permute-start | bytes 18440 | tf_op jit(solution)/shard_map/ppermute | solution.py:64
  21.3 0.9 copy.10
  22.2 1.1 reshape.293
  23.4 0.9 reduce_sum.18
  24.3 1.7 %convolution_multiply_fusion.1 = f32[256,128]{0,1:T(8,128)S(1)} fusion(f32[256,512]{1,0:T(8,128)} %reduce_sum.18, f32[512,128]{0,1:T(8,128)S(1)} %reshape.293), kind=kOutput, calls=%fused_computation.33 | convolution fusion | flops 201359360 | bytes 917504 | tf_op jit(solution)/shard_map/dot_general | solution.py:155
  26.7 11.8 %all-to-all-start = ((f32[32,256,4]{1,2,0:T(4,128)}), f32[32,256,4]{1,2,0:T(4,128)S(1)}, u32[]{:S(2)}, u32[]{:S(2)}) async-start(f32[32,256,4]{1,2,0:T(4,128)} %bitcast.61), calls=%async_computation | async-start | bytes 262144 | tf_op jit(solution)/shard_map/all_to_all | solution.py:19
  38.5 3.8 %pad_maximum_fusion.1 = f32[3,2,256,512]{3,2,1,0:T(8,128)} fusion(f32[1,2,256,512]{3,2,1,0:T(8,128)} %bitcast.52, f32[1,2,256,512]{3,2,1,0:T(8,128)} %bitcast.57, f32[1,2,256,512]{3,2,1,0:T(8,128)S(1)} %bitcast.47), kind=kLoop, calls=%fused_computation.19 | loop fusion | flops 1572864 | bytes 6291456 | tf_op jit(solution)/shard_map/stack | solution.py:178
  44.8 1.9 %copy.12 = f32[512,64,2]{0,2,1:T(2,128)} copy(f32[512,64,2]{0,1,2:T(8,128)} %get-tuple-element.46) | data formatting | bytes 524288 | tf_op jit(solution)/shard_map/stack | solution.py:78
  46.6 1.8 %reshape.298 = f32[512,128]{0,1:T(8,128)} reshape(f32[512,64,2]{0,2,1:T(2,128)} %copy.12) | data formatting | bytes 524288 | tf_op jit(solution)/shard_map/reshape | solution.py:80
  49.0 2.5 %maximum_convert_fusion = f32[3,2,256,514]{3,2,1,0:T(8,128)S(1)} fusion(bf16[3,2,256,1]{3,2,1,0:T(8,128)(2,1)} %collective-permute-done.3, bf16[3,2,256,512]{3,2,1,0:T(8,128)(2,1)} %copy-done.8, bf16[3,2,256,1]{3,2,1,0:T(8,128)(2,1)} %collective-permute-done.2), kind=kLoop, calls=%fused_computation.20 | loop fusion | flops 4737024 | bytes 4737024 | tf_op jit(solution)/shard_map/convert_element_type | solution.py:179
  51.5 1.4 %multiply_add_fusion = (f32[1,2,256,513]{3,2,1,0:T(8,128)S(1)}, f32[1,2,256,513]{3,2,1,0:T(8,128)S(1)}, f32[2,256,513]{2,1,0:T(8,128)S(1)}, f32[1,2,256,513]{3,2...) fusion(f32[3,2,256,514]{3,2,1,0:T(8,128)S(1)} %maximum_convert_, ...), kind=kLoop, calls=%fused_computation.24 | loop fusion | flops 3939840 | bytes 13660160 | tf_op jit(solution)/shard_map/add | solution.py:104
  53.0 2.5 %fusion.1 = f32[3,2,256,513]{3,2,1,0:T(8,128)} fusion(f32[3,2,256,514]{3,2,1,0:T(8,128)S(1)} %maximum_convert_fusion, f32[1,2,256,513]{3,2,1,0:T(8,128)S(1)} %get-tuple-element.11, f32[1,2,256,513]{3,2,1,0:T(8,128)S(1)} %get-tuple-element.15, f32[1,2,256,513]{3,2,1,0:T(8,128)S(1)} %get-tuple-element.16, f32[1,2,256,513]{3,2,1,0:T(8,128)S(1)} %get-tuple-element.10, ...), kind=kLoop, calls=%fused_computation.2 | loop fusion | flops 7091712 | bytes 16809984 | tf_op jit(solution)/shard_map/sub | solution.py:111
  56.1 1.0 broadcast_select_fusion
  57.7 3.1 %pad_maximum_fusion = (f32[3,2,257,512]{3,2,1,0:T(8,128)}, f32[3,2,257,512]{3,2,1,0:T(8,128)}) fusion(f32[3,2,1,512]{3,2,1,0:T(1,128)S(1)} %get-tuple-element.8, f32[1,2,256,512]{3,2,1,0:T(8,128)S(1)} %bitcast.54, f32[1,2,256,512]{3,2,1,0:T(8,128)S(1)} %bitcast.59, f32[1,2,256,512]{3,2,1,0:T(8,128)S(1)} %bitcast.48, f32[3,2,1,512]{3,2,1,0:T(1,128)S(1)} %get-tuple-element.9), kind=kLoop, calls=%fused_computation.10 | loop fusion | flops 4737024 | bytes 9486336 | tf_op jit(solution)/shard_map/concatenate | solution.py:187
  61.5 1.3 %broadcast_in_dim.2 = bf16[8,256,4]{1,2,0:T(4,128)(2,1)} broadcast(bf16[256,4]{0,1:T(4,128)(2,1)} %reduce_sum.19), dimensions={1,2} | broadcast | bytes 18432 | tf_op jit(solution)/shard_map/broadcast_in_dim | solution.py:32
  62.8 4.8 %all-to-all-start.1 = ((bf16[8,256,4]{1,2,0:T(4,128)(2,1)}), bf16[8,256,4]{1,2,0:T(4,128)(2,1)S(1)}, u32[]{:S(2)}, u32[]{:S(2)}) async-start(bf16[8,256,4]{1,2,0:T(4,128)(2,1)} %broadcast_in_dim.2), calls=%async_computation.1 | async-start | bytes 32768 | tf_op jit(solution)/shard_map/all_to_all | solution.py:31
  67.6 7.3 %multiply_bitcast_fusion.1 = (f32[2,257,512]{2,1,0:T(8,128)}, f32[1,2,257,512]{3,2,1,0:T(8,128)}, f32[1,2,257,512]{3,2,1,0:T(8,128)}, f32[1,2,257,512]{3,2,1,0:T...) fusion(f32[257]{0:T(512)} %get-tuple-element.44, ...), kind=kLoop, calls=%fused_computation.38 | loop fusion | flops 3947520 | bytes 13686792 | tf_op jit(solution)/shard_map/mul | solution.py:96
  75.6 2.2 %convolution_bitcast_fusion.1 = f32[256,2,2]{0,2,1:T(2,128)S(1)} fusion(bf16[2048,2,2]{0,2,1:T(2,128)(2,1)S(1)} %reshape_reshape.3, bf16[2,256,2048]{2,1,0:T(8,128)(2,1)} %param.8), kind=kOutput, calls=%fused_computation.35 | convolution fusion | flops 4194304 | bytes 2117632 | tf_op jit(solution)/shard_map/krs,skc->rkc/dot_general | solution.py:161
  78.6 12.5 %all-to-all-start.2 = ((f32[32,4,512]{2,1,0:T(4,128)}), f32[32,4,512]{2,1,0:T(4,128)}, u32[]{:S(2)}, u32[]{:S(2)}) async-start(f32[32,4,512]{2,1,0:T(4,128)} %stack.33), calls=%async_computation.2 | async-start | bytes 524288 | tf_op jit(solution)/shard_map/all_to_all | solution.py:45
  91.2 7.4 %fusion.5 = f32[3,2,257,512]{3,2,1,0:T(8,128)} fusion(f32[1,2,257,512]{3,2,1,0:T(8,128)} %get-tuple-element.22, f32[1,2,257,512]{3,2,1,0:T(8,128)} %get-tuple-element.19, f32[1,2,257,512]{3,2,1,0:T(8,128)} %get-tuple-element.23, f32[1,2,257,512]{3,2,1,0:T(8,128)} %get-tuple-element.20, f32[1,2,257,512]{3,2,1,0:T(8,128)} %get-tuple-element.18, ...), kind=kLoop, calls=%fused_computation.9 | loop fusion | flops 12632064 | bytes 13698052 | tf_op jit(solution)/shard_map/mul | solution.py:123
  98.6 8.4 %all-to-all-done.2 = f32[32,4,512]{2,1,0:T(4,128)} async-done(((f32[32,4,512]{2,1,0:T(4,128)}), f32[32,4,512]{2,1,0:T(4,128)}, u32[]{:S(2)}, u32[]{:S(2)}) %all-to-all-start.2) | async-done | bytes 262176 | tf_op jit(solution)/shard_map/all_to_all | solution.py:45
  107.0 1.7 %reshape.297 = f32[128,512]{1,0:T(8,128)} reshape(f32[32,4,512]{2,1,0:T(4,128)} %all-to-all-done.2) | data formatting | bytes 524288 | tf_op jit(solution)/shard_map/reshape | solution.py:44
  108.8 2.5 %fusion.16 = f32[256,512]{1,0:T(8,128)} fusion(f32[512,128]{0,1:T(8,128)S(1)} %reshape.293, f32[128,512]{1,0:T(8,128)} %reshape.297), kind=kOutput, calls=%fused_computation.53 | convolution fusion | flops 201326592 | bytes 917504 | tf_op jit(solution)/shard_map/dot_general | solution.py:170
  111.2 1.5 %fusion.14 = f32[256,512]{1,0:T(8,128)S(1)} fusion(f32[512,128]{0,1:T(8,128)S(1)} %reshape.293, f32[256]{0:T(256)S(1)} %copy-done.20, f32[128,512]{1,0:T(8,128)} %reshape.297), kind=kOutput, calls=%fused_computation.30 | convolution fusion | flops 201588736 | bytes 918528 | tf_op jit(solution)/shard_map/dot_general | solution.py:171
  112.8 1.8 %fusion.13 = f32[256,512]{1,0:T(8,128)S(1)} fusion(f32[512,128]{0,1:T(8,128)} %reshape.298, f32[256]{0:T(256)S(1)} %copy-done.16, f32[128,512]{1,0:T(8,128)} %reshape.297), kind=kOutput, calls=%fused_computation.28 | convolution fusion | flops 201719808 | bytes 918528 | tf_op jit(solution)/shard_map/dot_general | solution.py:172
  115.4 1.3 %copy-done.6 = f32[3,2,257,512]{3,2,1,0:T(8,128)S(1)} copy-done((f32[3,2,257,512]{3,2,1,0:T(8,128)S(1)}, f32[3,2,257,512]{3,2,1,0:T(8,128)}, u32[]{:S(2)}) %copy-start.6) | copy-done | bytes 3158040
  116.7 1.7 %fusion.10 = f32[3,2,256,512]{3,2,1,0:T(8,128)S(1)} fusion(f32[3,2,256,513]{3,2,1,0:T(8,128)S(1)} %copy-done.7, f32[3,2,257,512]{3,2,1,0:T(8,128)S(1)} %copy-done.6, f32[1,2,256,512]{3,2,1,0:T(8,128)S(1)} %get-tuple-element.30, f32[1,2,256,512]{3,2,1,0:T(8,128)S(1)} %get-tuple-element.29, f32[3]{0:T(128)S(1)} %copy-done.21, f32[256]{0:T(256)S(1)} %copy-done.19, ...), kind=kLoop, calls=%fused_computation.16 | loop fusion | flops 9437184 | bytes 20973580 | tf_op jit(solution)/shard_map/add | solution.py:138
  118.4 1.7 %slice_bitcast_fusion = (f32[2,256,512]{2,1,0:T(8,128)}, f32[2,256,512]{2,1,0:T(8,128)}, f32[2,256,512]{2,1,0:T(8,128)}) fusion(f32[3,2,256,512]{3,2,1,0:T(8,128)S(1)} %fusion.10), kind=kLoop, calls=%fused_computation.41 | loop fusion | bytes 6291456 | tf_op jit(solution)/shard_map/squeeze | solution.py:191
  (71 shorter events, 9.7 us)
Async XLA Ops:
  0.6 74.3 %copy-start = (bf16[2,256,2048]{2,1,0:T(8,128)(2,1)S(1)}, bf16[2,256,2048]{2,1,0:T(8,128)(2,1)}, u32[]{:S(2)}) copy-start(bf16[2,256,2048]{2,1,0:T(8,128)(2,1)} %param.9) | copy-start | bytes 6291460
  3.0 12.0 %copy-start.8 = (bf16[3,2,256,512]{3,2,1,0:T(8,128)(2,1)}, bf16[3,2,256,512]{3,2,1,0:T(8,128)(2,1)S(1)}, u32[]{:S(2)}) copy-start(bf16[3,2,256,512]{3,2,1,0:T(8,128)(2,1)S(1)} %fusion.22) | copy-start | bytes 4718596
  3.0 20.3 %copy-start.1 = (f32[2,256,512]{2,1,0:T(8,128)S(1)}, f32[2,256,512]{2,1,0:T(8,128)}, u32[]{:S(2)}) copy-start(f32[2,256,512]{2,1,0:T(8,128)} %param.5) | copy-start | bytes 3145732
  4.1 44.9 %collective-permute-start.3 = (bf16[3,2,256,1]{3,2,1,0:T(8,128)(2,1)}, bf16[3,2,256,1]{3,2,1,0:T(8,128)(2,1)}, u32[]{:S(2)}, u32[]{:S(2)}) collective-permute-start(bf16[3,2,256,1]{3,2,1,0:T(8,128)(2,1)} %get-tuple-element.34), channel_id=1, source_target_pairs={{8,0},{16,8},{24,16},{32,24},{40,32},{48,40},{56,48},{64,56},{72,6... | collective-permute-start | bytes 9224 | tf_op jit(solution)/shard_map/ppermute | solution.py:67
  15.0 34.0 %collective-permute-start.2 = (bf16[3,2,256,1]{3,2,1,0:T(8,128)(2,1)}, bf16[3,2,256,1]{3,2,1,0:T(8,128)(2,1)}, u32[]{:S(2)}, u32[]{:S(2)}) collective-permute-start(bf16[3,2,256,1]{3,2,1,0:T(8,128)(2,1)} %get-tuple-element.33), channel_id=1, source_target_pairs={{0,8},{8,16},{16,24},{24,32},{32,40},{40,48},{48,56},{56,64},{64,7... | collective-permute-start | bytes 9224 | tf_op jit(solution)/shard_map/ppermute | solution.py:64
  15.6 39.8 %collective-permute-start.1 = (bf16[3,2,1,512]{3,2,1,0:T(2,128)(2,1)}, bf16[3,2,1,512]{3,2,1,0:T(2,128)(2,1)S(1)}, u32[]{:S(2)}, u32[]{:S(2)}) collective-permute-start(bf16[3,2,1,512]{3,2,1,0:T(2,128)(2,1)} %get-tuple-element.32), channel_id=1, source_target_pairs={{1,0},{2,1},{3,2},{4,3},{5,4},{6,5},{7,6},{9,8},{10,9},{11,10},{12... | collective-permute-start | bytes 18440 | tf_op jit(solution)/shard_map/ppermute | solution.py:67
  17.7 38.4 %collective-permute-start = (bf16[3,2,1,512]{3,2,1,0:T(2,128)(2,1)}, bf16[3,2,1,512]{3,2,1,0:T(2,128)(2,1)}, u32[]{:S(2)}, u32[]{:S(2)}) collective-permute-start(bf16[3,2,1,512]{3,2,1,0:T(2,128)(2,1)} %get-tuple-element.31), channel_id=1, source_target_pairs={{0,1},{1,2},{2,3},{3,4},{4,5},{5,6},{6,7},{8,9},{9,10},{10,11},{11... | collective-permute-start | bytes 18440 | tf_op jit(solution)/shard_map/ppermute | solution.py:64
  26.7 34.2 %all-to-all-start = ((f32[32,256,4]{1,2,0:T(4,128)}), f32[32,256,4]{1,2,0:T(4,128)S(1)}, u32[]{:S(2)}, u32[]{:S(2)}) async-start(f32[32,256,4]{1,2,0:T(4,128)} %bitcast.61), calls=%async_computation | async-start | bytes 262144 | tf_op jit(solution)/shard_map/all_to_all | solution.py:19
  43.0 0.6 copy-start.15
  49.0 2.5 %copy-start.13 = (f32[256]{0:T(256)S(1)}, f32[256]{0:T(256)}, u32[]{:S(2)}) copy-start(f32[256]{0:T(256)} %get-tuple-element.7) | copy-start | bytes 3076
  49.0 2.5 %copy-start.17 = (f32[256]{0:T(256)S(1)}, f32[256]{0:T(256)}, u32[]{:S(2)}) copy-start(f32[256]{0:T(256)} %get-tuple-element.6) | copy-start | bytes 3076
  52.9 3.1 %copy-start.9 = (bf16[3,2,256,512]{3,2,1,0:T(8,128)(2,1)S(1)}, bf16[3,2,256,512]{3,2,1,0:T(8,128)(2,1)}, u32[]{:S(2)}) copy-start(bf16[3,2,256,512]{3,2,1,0:T(8,128)(2,1)} %copy-done.8) | copy-start | bytes 4718596
  52.9 4.8 %copy-start.2 = (f32[2,256,512]{2,1,0:T(8,128)S(1)}, f32[2,256,512]{2,1,0:T(8,128)}, u32[]{:S(2)}) copy-start(f32[2,256,512]{2,1,0:T(8,128)} %param.7) | copy-start | bytes 3145732
  53.0 4.8 %copy-start.4 = (f32[2,256,512]{2,1,0:T(8,128)S(1)}, f32[2,256,512]{2,1,0:T(8,128)}, u32[]{:S(2)}) copy-start(f32[2,256,512]{2,1,0:T(8,128)} %param.6) | copy-start | bytes 3145732
  55.5 0.6 copy-start.12
  57.1 0.6 copy-start.10
  62.8 12.1 %all-to-all-start.1 = ((bf16[8,256,4]{1,2,0:T(4,128)(2,1)}), bf16[8,256,4]{1,2,0:T(4,128)(2,1)S(1)}, u32[]{:S(2)}, u32[]{:S(2)}) async-start(bf16[8,256,4]{1,2,0:T(4,128)(2,1)} %broadcast_in_dim.2), calls=%async_computation.1 | async-start | bytes 32768 | tf_op jit(solution)/shard_map/all_to_all | solution.py:31
  74.8 16.3 %copy-start.11 = (f32[3,2,1,512]{3,2,1,0:T(1,128)S(1)}, f32[3,2,1,512]{3,2,1,0:T(1,128)}, u32[]{:S(2)}) copy-start(f32[3,2,1,512]{3,2,1,0:T(1,128)} %copy-done.10) | copy-start | bytes 36868
  78.6 28.4 %all-to-all-start.2 = ((f32[32,4,512]{2,1,0:T(4,128)}), f32[32,4,512]{2,1,0:T(4,128)}, u32[]{:S(2)}, u32[]{:S(2)}) async-start(f32[32,4,512]{2,1,0:T(4,128)} %stack.33), calls=%async_computation.2 | async-start | bytes 524288 | tf_op jit(solution)/shard_map/all_to_all | solution.py:45
  91.1 20.1 %copy-start.20 = (f32[256]{0:T(256)S(1)}, f32[256]{0:T(256)}, u32[]{:S(2)}) copy-start(f32[256]{0:T(256)} %get-tuple-element.41) | copy-start | bytes 3076
  91.2 21.6 %copy-start.16 = (f32[256]{0:T(256)S(1)}, f32[256]{0:T(256)}, u32[]{:S(2)}) copy-start(f32[256]{0:T(256)} %copy-done.15) | copy-start | bytes 3076
  98.6 16.0 %copy-start.14 = (f32[256]{0:T(256)S(1)}, f32[256]{0:T(256)}, u32[]{:S(2)}) copy-start(f32[256]{0:T(256)} %get-tuple-element.7) | copy-start | bytes 3076
  108.7 5.9 %copy-start.3 = (f32[2,256,512]{2,1,0:T(8,128)S(1)}, f32[2,256,512]{2,1,0:T(8,128)}, u32[]{:S(2)}) copy-start(f32[2,256,512]{2,1,0:T(8,128)} %param.7) | copy-start | bytes 3145732
  108.8 5.9 %copy-start.5 = (f32[2,256,512]{2,1,0:T(8,128)S(1)}, f32[2,256,512]{2,1,0:T(8,128)}, u32[]{:S(2)}) copy-start(f32[2,256,512]{2,1,0:T(8,128)} %param.6) | copy-start | bytes 3145732
  112.8 2.6 %copy-start.7 = (f32[3,2,256,513]{3,2,1,0:T(8,128)S(1)}, f32[3,2,256,513]{3,2,1,0:T(8,128)}, u32[]{:S(2)}) copy-start(f32[3,2,256,513]{3,2,1,0:T(8,128)} %fusion.1) | copy-start | bytes 9455620
  114.6 2.0 %copy-start.6 = (f32[3,2,257,512]{3,2,1,0:T(8,128)S(1)}, f32[3,2,257,512]{3,2,1,0:T(8,128)}, u32[]{:S(2)}) copy-start(f32[3,2,257,512]{3,2,1,0:T(8,128)} %fusion.5) | copy-start | bytes 9474052
  114.6 2.0 %copy-start.18 = (f32[256]{0:T(256)S(1)}, f32[256]{0:T(256)}, u32[]{:S(2)}) copy-start(f32[256]{0:T(256)} %get-tuple-element.39) | copy-start | bytes 3076
  114.6 2.0 %copy-start.19 = (f32[256]{0:T(256)S(1)}, f32[256]{0:T(256)}, u32[]{:S(2)}) copy-start(f32[256]{0:T(256)} %get-tuple-element.40) | copy-start | bytes 3076
  114.7 2.0 %copy-start.21 = (f32[3]{0:T(128)S(1)}, f32[3]{0:T(128)}, u32[]{:S(2)}) copy-start(f32[3]{0:T(128)} %pad.26.clone) | copy-start | bytes 40
